TPU v7x, 32 devices: a whole 2x2x4 slice. The times are simulated.
32 devices in a mesh: groups: 1, expert: 16 (over z, y, core), head: 2 (over x).
Axes of the slice: x: 2, y: 2, z: 4, core: 2. Of those that a mesh axis runs over, the one named last changes fastest.
Arguments:
- tokens: bfloat16 [4096, 1024], P(('groups', 'expert')), may hold values from -6 to 6
- router: bfloat16 [1024, 16], replicated, may hold values from -0.1875 to 0.1875
- routes: int32 [4096, 2], P(('groups', 'expert')), may hold values from 0 to 15, all different within a row; in each aligned block of 256 rows (0 to 255, 256 to 511, ...) at most 48 rows name the same one
- w_in: bfloat16 [16, 1024, 4096], P('expert', None, 'head'), may hold values from -0.1875 to 0.1875
- w_out: bfloat16 [16, 4096, 1024], P('expert', 'head'), may hold values from -0.125 to 0.125
- lengths: int32 [32], P(('groups', 'expert')), may hold values from 1 to 128, 3072 in all
- kv_weight: bfloat16 [1024, 2, 1024], P('expert', None, 'head'), may hold values from -0.1875 to 0.1875
Outputs:
- kv: bfloat16 [4096, 2, 1024], P(('groups', 'expert'), None, 'head')
Inputs may be any that keep to these rules, and one draw needn't show every extreme that they name: `routes`: each row names two different experts; within the rows of one index of expert, aligned blocks of 256 rows, no expert is named more than 48 times, a bound that some block reaches. The lengths sum to 3072 and the largest is exactly 128.
All inputs are finite; a program needn't handle non-finite values. No bound on the sum of `lengths` on one device may be relied on, other than what follows from the above.
Results may differ from a plain program's by a relative error of at most 0.019.
Values may be sent and summed in bfloat16 or wider, within the bound.
A program may use at most 64 MiB of HBM per device.

v0:
```python
import jax
import jax.numpy as jnp
from jax import lax
from jax.sharding import PartitionSpec as P

QCOL = 256
SLEN = 128


def layer_norm(values):
    wide = values.astype(jnp.float32)
    center = jnp.mean(wide, axis=-1, keepdims=True)
    spread = jnp.mean((wide - center) ** 2, axis=-1, keepdims=True)
    return ((wide - center) * lax.rsqrt(spread + 1e-05)).astype(jnp.bfloat16)


def body(tokens, router, routes, w_in, w_out, lengths, kv_weight):
    n_head = lax.axis_size("head")
    head_at = lax.axis_index("head")
    count = tokens.shape[0]
    width = tokens.shape[1]
    quarter = width // n_head
    experts_all = router.shape[1]
    capacity = 3 * count // experts_all
    normed = layer_norm(tokens)
    logits = jnp.dot(normed, router, preferred_element_type=jnp.float32)
    flat_ids = routes.reshape(-1)
    onehot = (flat_ids[:, None] == jnp.arange(experts_all, dtype=jnp.int32)[None, :]).astype(
        jnp.int32
    )
    before = jnp.cumsum(onehot, axis=0) - onehot
    slot = jnp.sum(before * onehot, axis=1)
    chosen = jnp.sum(
        logits[:, None, :] * onehot.reshape(count, 2, experts_all).astype(jnp.float32), axis=2
    )
    first = 1.0 / (1.0 + jnp.exp(chosen[:, 1] - chosen[:, 0]))
    gates = jnp.stack([first, 1.0 - first], axis=1)
    position = flat_ids * capacity + slot
    repeated = jnp.repeat(normed, 2, axis=0)
    outgoing = jnp.zeros((experts_all * capacity, width), jnp.bfloat16).at[position].set(repeated)
    outgoing = outgoing.reshape(experts_all, capacity, width)
    first_w = w_in[0]
    second_w = w_out[0]
    received = lax.all_to_all(outgoing, "expert", split_axis=0, concat_axis=0, tiled=True)
    sources, items, _ = received.shape
    rows = received.reshape(sources * items, width)
    hidden = jax.nn.relu(jnp.dot(rows, first_w, preferred_element_type=jnp.float32)).astype(
        jnp.bfloat16
    )
    partial_value = jnp.dot(hidden, second_w, preferred_element_type=jnp.float32).reshape(
        sources, items, width
    )
    summed = lax.psum_scatter(partial_value, "head", scatter_dimension=2, tiled=True)
    back = lax.all_to_all(
        summed.astype(jnp.bfloat16), "expert", split_axis=0, concat_axis=0, tiled=True
    )
    picked = (
        back.reshape(experts_all * capacity, quarter)[position]
        .reshape(count, 2, quarter)
        .astype(jnp.float32)
    )
    own_cols = lax.dynamic_slice_in_dim(tokens, head_at * quarter, quarter, 1).astype(jnp.float32)
    encoded = own_cols + jnp.sum(gates[:, :, None] * picked, axis=1)
    grouped = encoded.reshape(count, quarter // QCOL, QCOL)
    scales = (jnp.max(jnp.abs(grouped), axis=2) / 127.0 + 1e-06).astype(jnp.bfloat16)
    coded = jnp.floor(grouped / scales.astype(jnp.float32)[:, :, None] + 0.5)
    scaled = jnp.clip(coded, -127.0, 127.0).astype(jnp.bfloat16).reshape(count, quarter)
    scaled_all, scales_all = (
        lax.all_gather(scaled, "head", axis=1, tiled=True),
        lax.all_gather(scales, "head", axis=1, tiled=True),
    )
    restored = (
        scaled_all.reshape(count, width // QCOL, QCOL).astype(jnp.float32)
        * scales_all.astype(jnp.float32)[:, :, None]
    )
    restored = restored.astype(jnp.bfloat16).reshape(count, width)
    projected = jnp.einsum(
        "td,dcj->tcj",
        restored,
        lax.all_gather(kv_weight, "expert", axis=0, tiled=True),
        preferred_element_type=jnp.float32,
    )
    place = jnp.arange(count, dtype=jnp.int32)
    sentence = place // SLEN
    pick_len = (sentence[:, None] == jnp.arange(lengths.shape[0], dtype=jnp.int32)[None, :]).astype(
        jnp.int32
    )
    limit = jnp.sum(pick_len * lengths[None, :], axis=1)
    keep = (place % SLEN < limit).astype(jnp.float32)
    return (projected * keep[:, None, None]).astype(jnp.bfloat16)


def solution(mesh):
    placed = (
        P(("groups", "expert"), None),
        P(),
        P(("groups", "expert"), None),
        P("expert", None, "head"),
        P("expert", "head", None),
        P(("groups", "expert")),
        P("expert", None, "head"),
    )
    return jax.shard_map(
        body,
        mesh=mesh,
        in_specs=placed,
        out_specs=P(("groups", "expert"), None, "head"),
        check_vma=False,
    )
```

profile of v0, /device:TPU:16, one launch (start us, length us, event | category | flops | bytes accessed | tf_op | source)
XLA Modules:
  0.0 172.4 jit_solution(15093324059837816524)
XLA Ops:
  7.4 0.8 copy.45
  8.5 0.7 broadcast_multiply_fusion
  9.2 1.1 reduce-window.6
  10.9 1.2 convert_reduce_fusion
  12.1 1.3 fusion.9
  13.4 1.3 fusion.10
  14.7 0.5 broadcast_in_dim.5
  15.8 3.0 %scatter_custom_fusion = bf16[768,1024]{1,0:T(8,128)(2,1)S(1)} fusion(s32[512]{0:T(512)S(1)} %bitcast.59, bf16[512,1024]{1,0:T(8,128)(2,1)S(1)} %reshape.145, bf16[]{:T(256)} %constant.64.clone.1), kind=kCustom, calls=%fused_computation.17 | custom fusion | bytes 1572866 | tf_op jit(solution)/shard_map/scatter | solution.py:40
  18.9 42.3 %all_to_all.10 = bf16[16,48,1024]{2,1,0:T(8,128)(2,1)S(1)} all-to-all(bf16[16,48,1024]{2,1,0:T(8,128)(2,1)S(1)} %bitcast.52), channel_id=1, replica_groups=mesh['groups'=1,'expert'=16,'head'=2] {'expert'}, dimensions={0} | all-to-all | bytes 3145728 | tf_op jit(solution)/shard_map/all_to_all | solution.py:44
  61.2 5.9 %maximum_convert_fusion = bf16[768,2048]{1,0:T(8,128)(2,1)S(1)} fusion(bf16[768,1024]{1,0:T(8,128)(2,1)S(1)} %bitcast.57, bf16[1,1024,2048]{2,1,0:T(8,128)(2,1)} %param.10), kind=kOutput, calls=%fused_computation.2 | convolution fusion | flops 3224371200 | bytes 8912896 | tf_op jit(solution)/shard_map/dot_general | solution.py:47
  67.2 5.1 %fusion = f32[16,48,1024]{2,1,0:T(8,128)} fusion(bf16[16,48,2048]{2,1,0:T(8,128)(2,1)S(1)} %bitcast.62, bf16[1,2048,1024]{2,1,0:T(8,128)(2,1)S(1)} %copy-done.5), kind=kOutput, calls=%fused_computation.3 | convolution fusion | flops 3221225472 | bytes 10485760 | tf_op jit(solution)/shard_map/dot_general | solution.py:50
  72.3 0.8 copy-done.2
  73.1 0.7 copy.51
  73.8 41.6 %reduce-scatter.2.cloned.1.call-done = f32[16,48,512]{2,1,0:T(8,128)} async-done(((f32[16,48,1024]{2,1,0:T(8,128)}), f32[16,48,512]{2,1,0:T(8,128)}) %reduce-scatter.2.cloned.1.call-update) | async-done | bytes 1572880 | tf_op jit(solution)/shard_map/reduce_scatter | solution.py:53
  115.4 2.4 %convert_element_type.82 = bf16[16,48,512]{2,1,0:T(8,128)(2,1)} convert(f32[16,48,512]{2,1,0:T(8,128)} %reduce-scatter.2.cloned.1.call-done) | non-fusion elementwise | flops 393216 | bytes 2359296 | tf_op jit(solution)/shard_map/convert_element_type | solution.py:55
  117.8 6.0 %all-to-all-start.1 = ((bf16[16,48,512]{2,1,0:T(8,128)(2,1)}), bf16[16,48,512]{2,1,0:T(8,128)(2,1)S(1)}, u32[]{:S(2)}, u32[]{:S(2)}) async-start(bf16[16,48,512]{2,1,0:T(8,128)(2,1)} %convert_element_type.82), calls=%async_computation.2 | async-start | bytes 1572864 | tf_op jit(solution)/shard_map/all_to_all | solution.py:54
  124.5 19.0 %all-to-all-done.1 = bf16[16,48,512]{2,1,0:T(8,128)(2,1)S(1)} async-done(((bf16[16,48,512]{2,1,0:T(8,128)(2,1)}), bf16[16,48,512]{2,1,0:T(8,128)(2,1)S(1)}, u32[]{:S(2)}, u32[]{:S(2)}) %all-to-all-start.1) | async-done | bytes 786464 | tf_op jit(solution)/shard_map/all_to_all | solution.py:54
  143.4 2.0 %gather_fusion = bf16[512,512]{1,0:T(8,128)(2,1)S(1)} fusion(bf16[768,512]{1,0:T(8,128)(2,1)S(1)} %bitcast.51, s32[1024]{0:T(1024)S(1)} %pad_clamp_fusion), kind=kCustom, calls=%fused_computation | custom fusion | bytes 1050624 | tf_op jit(solution)/shard_map/gather | solution.py:58
  145.4 0.7 reshape.132
  146.0 1.3 multiply_reduce_fusion
  148.8 4.2 %all-gather = bf16[2,2,256]{2,1,0:T(2,128)(2,1)S(1)} all-gather(bf16[1,2,256]{2,1,0:T(2,128)(2,1)S(1)} %get-tuple-element.8), channel_id=1, replica_groups=mesh['groups'=1,'expert'=16,'head'=2] {'head'}, dimensions={0}, use_global_device_ids=true | all-gather | bytes 3072 | tf_op jit(solution)/shard_map/all_gather | solution.py:70
  153.9 7.4 %all_gather.9 = bf16[256,1024]{1,0:T(8,128)(2,1)S(1)} all-gather(bf16[256,512]{1,0:T(8,128)(2,1)S(1)} %clamp_convert_fusion), channel_id=1, replica_groups=mesh['groups'=1,'expert'=16,'head'=2] {'head'}, dimensions={1}, use_global_device_ids=true | all-gather | bytes 786432 | tf_op jit(solution)/shard_map/all_gather | solution.py:69
  161.3 2.3 %fusion.6 = bf16[256,2,512]{2,0,1:T(8,128)(2,1)S(1)} fusion(bf16[1024,2,512]{2,0,1:T(8,128)(2,1)} %all-gather.3.cloned.1.call-done, f32[256,1024]{1,0:T(8,128)S(1)} %bitcast.53, bf16[256,1024]{1,0:T(8,128)(2,1)S(1)} %all_gather.9, f32[256]{0:T(256)S(1)} %compare_convert_fusion), kind=kOutput, calls=%fused_computation.10 | convolution fusion | flops 538181632 | bytes 4195328 | tf_op jit(solution)/shard_map/td,dcj->tcj/dot_general | solution.py:77
  163.6 1.3 copy.52
  (51 shorter events, 4.3 us)
Async XLA Ops:
  7.4 116.5 %copy-start = (bf16[1024,16]{0,1:T(8,128)(2,1)S(1)}, bf16[1024,16]{0,1:T(8,128)(2,1)}, u32[]{:S(2)}) copy-start(bf16[1024,16]{0,1:T(8,128)(2,1)} %param.8) | copy-start | bytes 98308
  7.4 108.0 %reduce-scatter.2.cloned.1.call-start = ((), (), s32[]{:S(2)}) async-start(), calls=%async_computation.3 | async-start | bytes 4718592 | tf_op jit(solution)/shard_map/reduce_scatter | solution.py:53
  61.2 6.0 %copy-start.5 = (bf16[1,2048,1024]{2,1,0:T(8,128)(2,1)S(1)}, bf16[1,2048,1024]{2,1,0:T(8,128)(2,1)}, u32[]{:S(2)}) copy-start(bf16[1,2048,1024]{2,1,0:T(8,128)(2,1)} %param.11) | copy-start | bytes 12582916
  72.2 0.9 copy-start.2
  72.3 51.8 %copy-start.3 = (s32[256,2]{0,1:T(2,128)S(1)}, s32[256,2]{0,1:T(2,128)}, u32[]{:S(2)}) copy-start(s32[256,2]{0,1:T(2,128)} %param.9) | copy-start | bytes 6148
  72.3 52.1 %copy-start.4 = (s32[2]{0:T(128)S(1)}, s32[2]{0:T(128)}, u32[]{:S(2)}) copy-start(s32[2]{0:T(128)} %param.12) | copy-start | bytes 28
  72.3 89.0 %all-gather.3.cloned.1.call-start = ((), (), s32[]{:S(2)}) async-start(), calls=%async_computation.4 | async-start | bytes 2228224 | tf_op jit(solution)/shard_map/all_gather | solution.py:80
  117.8 25.6 %all-to-all-start.1 = ((bf16[16,48,512]{2,1,0:T(8,128)(2,1)}), bf16[16,48,512]{2,1,0:T(8,128)(2,1)S(1)}, u32[]{:S(2)}, u32[]{:S(2)}) async-start(bf16[16,48,512]{2,1,0:T(8,128)(2,1)} %convert_element_type.82), calls=%async_computation.2 | async-start | bytes 1572864 | tf_op jit(solution)/shard_map/all_to_all | solution.py:54
  143.4 4.0 %copy-start.1 = (bf16[256,1024]{1,0:T(8,128)(2,1)S(1)}, bf16[256,1024]{1,0:T(8,128)(2,1)}, u32[]{:S(2)}) copy-start(bf16[256,1024]{1,0:T(8,128)(2,1)} %param.7) | copy-start | bytes 1572868
Sparse Core Ops, SparseCore 0:
  72.4 42.9 reduce-scatter.1
Sparse Core Ops, SparseCore 1:
  75.0 39.3 all-gather.2
where the time goes:
time: 174 us; the launch traced here: 172 us
  waiting for transfers between devices  60.6 us (35%)
  blocking collectives  54 us (31%)
  between operations  15.1 us (9%)
  matrix products  13.6 us (8%)
  local copies, waits for them, and re-layouts  12.8 us (7%)
  other arithmetic  10.3 us (6%)
  starting transfers between devices  6.09 us (4%)
    all_to_all x1, blocking collectives, body(): lax.all_to_all(outgoing, 'expert', split_axis=0, concat_axis=0, tiled=True)  42.3 us
    reduce_scatter x1, waiting for transfers between devices, body(): lax.psum_scatter(partial_value, 'head', scatter_dimension=2, tiled=True)  41.6 us
    all_to_all x1, waiting for transfers between devices, body(): lax.all_to_all(summed.astype(jnp.bfloat16), 'expert', split_axis=0, conca...  19 us
    all_gather x1, blocking collectives, body(): lax.all_gather(scaled, 'head', axis=1, tiled=True)  7.39 us
    all_to_all x1, starting transfers between devices, body(): lax.all_to_all(summed.astype(jnp.bfloat16), 'expert', split_axis=0, conca...  6.04 us
    dot_general x1, matrix products, body(): jnp.dot(rows, first_w, preferred_element_type=jnp.float32)  5.95 us
    dot_general x1, matrix products, body(): jnp.dot(hidden, second_w, preferred_element_type=jnp.float32)  5.08 us
    all_gather x1, blocking collectives, body(): lax.all_gather(scales, 'head', axis=1, tiled=True)  4.25 us
  transfers between devices with their start and end apart: 3, of which 2 were waited for; matrix products, arithmetic and copies ran while one was open for 6% of the time, Pallas kernels for 0%

commit v1 on v0

v1 whole, which is shorter than its diff:
```python
import functools

import jax
import jax.numpy as jnp
from jax import lax
from jax.experimental import pallas as pl
from jax.experimental.pallas import tpu as pltpu
from jax.sharding import PartitionSpec as P

QCOL = 256
SLEN = 128
MESH = pl.DeviceIdType.MESH
F32 = jnp.float32
BF16 = jnp.bfloat16


def flip(me, k, n):
    out, bit = 0, 1
    while bit < n:
        a = lax.rem(lax.div(me, jnp.int32(bit)), jnp.int32(2))
        b = lax.rem(lax.div(jnp.int32(k), jnp.int32(bit)), jnp.int32(2))
        out = out + bit * lax.rem(a + b, jnp.int32(2))
        bit *= 2
    return out


def kernel(
    n, cap, groups,
    tokens_ref, router_ref, routes_ref, w_in_hbm, w_out_hbm, restored_ref,
    w_in, w_out, onehots, outgoing, rows_in, hidden, part_out, part_in, part_own, summed, back, coded,
    w_sem, disp_send, disp_recv, fwd_send, fwd_recv, red_send, red_recv, ret_send, ret_recv, code_send, code_recv,
):
    me = lax.axis_index("expert")
    head = lax.axis_index("head")
    other = 1 - head
    count, width = tokens_ref.shape
    half = width // 2
    ff = w_in.shape[1]
    block = n // groups * cap
    near = n // 2
    mine = pl.ds(pl.multiple_of(head * half, half), half)
    theirs = pl.ds(pl.multiple_of(other * half, half), half)

    load_in = pltpu.make_async_copy(w_in_hbm.at[0], w_in, w_sem.at[0])
    load_out = pltpu.make_async_copy(w_out_hbm.at[0], w_out, w_sem.at[1])
    load_in.start()
    load_out.start()

    barrier = pltpu.get_barrier_semaphore()

    @pl.loop(1, n)
    def _(k):
        pl.semaphore_signal(barrier, inc=1, device_id={"expert": flip(me, k, n)}, device_id_type=MESH)

    pl.semaphore_signal(barrier, inc=1, device_id={"head": other}, device_id_type=MESH)

    wide = tokens_ref[...].astype(F32)
    center = jnp.mean(wide, axis=-1, keepdims=True)
    spread = jnp.mean((wide - center) ** 2, axis=-1, keepdims=True)
    normed = ((wide - center) * lax.rsqrt(spread + 1e-05)).astype(BF16)
    logits = jnp.dot(normed, router_ref[...], preferred_element_type=F32)
    route0 = routes_ref[:, 0:1]
    route1 = routes_ref[:, 1:2]
    ids = lax.broadcasted_iota(jnp.int32, (count, n), 1)
    hot0 = (ids == route0).astype(F32)
    hot1 = (ids == route1).astype(F32)
    earlier = (
        lax.broadcasted_iota(jnp.int32, (count, count), 1) < lax.broadcasted_iota(jnp.int32, (count, count), 0)
    ).astype(F32).astype(BF16)
    before = jnp.dot(earlier, (hot0 + hot1).astype(BF16), preferred_element_type=F32)
    slot0 = jnp.sum(before * hot0, axis=1, keepdims=True).astype(jnp.int32)
    slot1 = jnp.sum(before * hot1, axis=1, keepdims=True).astype(jnp.int32)
    chosen0 = jnp.sum(logits * hot0, axis=1, keepdims=True)
    chosen1 = jnp.sum(logits * hot1, axis=1, keepdims=True)
    gate0 = 1.0 / (1.0 + jnp.exp(chosen1 - chosen0))
    gate1 = 1.0 - gate0
    place0 = jnp.bitwise_xor(route0, me) * cap + slot0
    place1 = jnp.bitwise_xor(route1, me) * cap + slot1
    columns = lax.broadcasted_iota(jnp.int32, (count, n * cap), 1)
    at0 = columns == place0
    at1 = columns == place1
    onehots[...] = jnp.where(at0 | at1, 1.0, 0.0).astype(BF16)

    def packed(first, last):
        picks = onehots[:, first * cap : last * cap]
        outgoing[first * cap : last * cap, :] = lax.dot_general(
            picks, normed, (((0,), (0,)), ((), ())), preferred_element_type=F32
        ).astype(BF16)

    def at(k):
        return pl.ds(pl.multiple_of(k * cap, cap), cap)

    def far_copy(k):
        return pltpu.make_async_remote_copy(
            src_ref=outgoing.at[at(k), mine], dst_ref=rows_in.at[at(k), mine],
            send_sem=disp_send.at[k], recv_sem=disp_recv.at[k],
            device_id={"expert": flip(me, k, n)}, device_id_type=MESH,
        )

    def near_copy(k):
        return pltpu.make_async_remote_copy(
            src_ref=outgoing.at[at(k)], dst_ref=rows_in.at[at(k)],
            send_sem=disp_send.at[k], recv_sem=disp_recv.at[k],
            device_id={"expert": flip(me, k, n)}, device_id_type=MESH,
        )

    packed(near, n)
    pl.semaphore_wait(barrier, n)

    @pl.loop(near, n)
    def _(k):
        far_copy(k).start()

    packed(0, near)

    @pl.loop(1, near)
    def _(k):
        near_copy(k).start()

    rows_in[0:cap, :] = outgoing[0:cap, :]

    low = jnp.where(at0, gate0, jnp.where(at1, gate1, 0.0))
    onehots[...] = low.astype(BF16)
    rest = (low - low.astype(BF16).astype(F32)).astype(BF16)

    per = n // groups

    def span(g):
        return slice(g * block, (g + 1) * block)

    def forward_copy(g):
        return pltpu.make_async_remote_copy(
            src_ref=rows_in.at[span(g), mine], dst_ref=rows_in.at[span(g), mine],
            send_sem=fwd_send.at[g], recv_sem=fwd_recv.at[g],
            device_id={"head": other}, device_id_type=MESH,
        )

    def reduce_copy(g):
        return pltpu.make_async_remote_copy(
            src_ref=part_out.at[span(g)], dst_ref=part_in.at[span(g)],
            send_sem=red_send.at[g], recv_sem=red_recv.at[g],
            device_id={"head": other}, device_id_type=MESH,
        )

    def return_copy(k):
        return pltpu.make_async_remote_copy(
            src_ref=summed.at[at(k)], dst_ref=back.at[at(k)],
            send_sem=ret_send.at[k], recv_sem=ret_recv.at[k],
            device_id={"expert": flip(me, k, n)}, device_id_type=MESH,
        )

    def arrive(g):
        far = g * per >= near

        @pl.loop(max(1, g * per), (g + 1) * per)
        def _(k):
            (far_copy if far else near_copy)(k).wait_recv()

        if far:
            forward_copy(g).start()

    def work(g):
        if g == 0:
            load_in.wait()
        if g * per >= near:
            forward_copy(g).wait_recv()
        tile = ff // 4

        @pl.loop(0, 4)
        def _(i):
            cols = pl.ds(pl.multiple_of(i * tile, tile), tile)
            value = jnp.dot(rows_in[span(g), :], w_in[:, cols], preferred_element_type=F32)
            hidden[:, cols] = jnp.maximum(value, 0.0).astype(BF16)

        if g == 0:
            load_out.wait()
        part_out[span(g), :] = jnp.dot(hidden[...], w_out[:, theirs], preferred_element_type=F32).astype(BF16)
        reduce_copy(g).start()
        part_own[span(g), :] = jnp.dot(hidden[...], w_out[:, mine], preferred_element_type=F32)

    def give(g):
        reduce_copy(g).wait_recv()
        summed[span(g), :] = (part_own[span(g), :] + part_in[span(g), :].astype(F32)).astype(BF16)
        if g == 0:
            back[0:cap, :] = summed[0:cap, :]

        @pl.loop(max(1, g * per), (g + 1) * per)
        def _(k):
            return_copy(k).start()

    arrive(0)
    work(0)
    arrive(1)
    for g in range(1, groups):
        if g + 1 < groups:
            arrive(g + 1)
        work(g)
        give(g - 1)
    give(groups - 1)

    @pl.loop(1, n)
    def _(k):
        return_copy(k).wait_recv()

    encoded = (
        tokens_ref[:, mine].astype(F32)
        + jnp.dot(onehots[...], back[...], preferred_element_type=F32)
        + jnp.dot(rest, back[...], preferred_element_type=F32)
    )
    for q in range(half // QCOL):
        part = encoded[:, q * QCOL : (q + 1) * QCOL]
        scale = (jnp.max(jnp.abs(part), axis=1, keepdims=True) / 127.0 + 1e-06).astype(BF16).astype(F32)
        whole = jnp.clip(jnp.floor(part / scale + 0.5), -127.0, 127.0)
        cols = pl.ds(pl.multiple_of(head * half + q * QCOL, QCOL), QCOL)
        coded[:, cols] = (whole * scale).astype(BF16)
    swap = pltpu.make_async_remote_copy(
        src_ref=coded.at[:, mine], dst_ref=coded.at[:, mine],
        send_sem=code_send, recv_sem=code_recv,
        device_id={"head": other}, device_id_type=MESH,
    )
    swap.start()

    @pl.loop(1, near)
    def _(k):
        near_copy(k).wait_send()

    @pl.loop(near, n)
    def _(k):
        far_copy(k).wait_send()

    @pl.loop(1, n)
    def _(k):
        return_copy(k).wait_send()

    for g in range(groups):
        if g * per >= near:
            forward_copy(g).wait_send()
        reduce_copy(g).wait_send()
    swap.wait()
    restored_ref[...] = coded[...]


def encoder(tokens, router, routes, w_in, w_out):
    n = lax.axis_size("expert")
    count, width = tokens.shape
    half = width // 2
    ff = w_in.shape[2]
    cap = -(-(3 * count // n) // 16) * 16
    groups = 4
    slots = n * cap
    vmem = pl.BlockSpec(memory_space=pltpu.VMEM)
    anywhere = pl.BlockSpec(memory_space=pl.ANY)
    dma = pltpu.SemaphoreType.DMA
    return pl.pallas_call(
        functools.partial(kernel, n, cap, groups),
        out_shape=jax.ShapeDtypeStruct((count, width), BF16),
        in_specs=[vmem, vmem, vmem, anywhere, anywhere],
        out_specs=vmem,
        scratch_shapes=[
            pltpu.VMEM((width, ff), BF16),
            pltpu.VMEM((ff, width), BF16),
            pltpu.VMEM((count, slots), BF16),
            pltpu.VMEM((slots, width), BF16),
            pltpu.VMEM((slots, width), BF16),
            pltpu.VMEM((slots // groups, ff), BF16),
            pltpu.VMEM((slots, half), BF16),
            pltpu.VMEM((slots, half), BF16),
            pltpu.VMEM((slots, half), F32),
            pltpu.VMEM((slots, half), BF16),
            pltpu.VMEM((slots, half), BF16),
            pltpu.VMEM((count, width), BF16),
            dma((2,)),
            dma((n,)), dma((n,)),
            dma((groups,)), dma((groups,)),
            dma((groups,)), dma((groups,)),
            dma((n,)), dma((n,)),
            dma, dma,
        ],
        compiler_params=pltpu.CompilerParams(
            collective_id=0, has_side_effects=True, vmem_limit_bytes=58 * 1024 * 1024
        ),
        cost_estimate=pl.CostEstimate(
            flops=4 * slots * width * ff, bytes_accessed=4 * width * ff, transcendentals=0
        ),
    )(tokens, router, routes, w_in, w_out)


def body(tokens, router, routes, w_in, w_out, lengths, kv_weight):
    count = tokens.shape[0]
    weight = lax.all_gather(kv_weight, "expert", axis=0, tiled=True)
    restored = encoder(tokens, router, routes, w_in, w_out)
    projected = jnp.einsum("td,dcj->tcj", restored, weight, preferred_element_type=F32)
    place = jnp.arange(count, dtype=jnp.int32)
    sentence = place // SLEN
    pick_len = (sentence[:, None] == jnp.arange(lengths.shape[0], dtype=jnp.int32)[None, :]).astype(
        jnp.int32
    )
    limit = jnp.sum(pick_len * lengths[None, :], axis=1)
    keep = (place % SLEN < limit).astype(F32)
    return (projected * keep[:, None, None]).astype(BF16)


def solution(mesh):
    placed = (
        P(("groups", "expert"), None),
        P(),
        P(("groups", "expert"), None),
        P("expert", None, "head"),
        P("expert", "head", None),
        P(("groups", "expert")),
        P("expert", None, "head"),
    )
    return jax.shard_map(
        body,
        mesh=mesh,
        in_specs=placed,
        out_specs=P(("groups", "expert"), None, "head"),
        check_vma=False,
    )
```

time: 174 us -> 99 us (0.57)
  Pallas kernels: 0 us -> 76 us
  waiting for transfers between devices: 60.6 us -> 0.04 us
  blocking collectives: 54 us -> 0 us
  matrix products: 13.6 us -> 2.48 us
  other arithmetic: 10.3 us -> 0.75 us
  local copies, waits for them, and re-layouts: 12.8 us -> 5.96 us
  starting transfers between devices: 6.09 us -> 0.01 us
    pallas_call x0 -> x1, Pallas kernels: none -> 76 us  [encoder(): pl.pallas_call(functools.partial(kernel, n, cap, groups), out_shape=jax.S...]
    all_to_all x1 -> x0, blocking collectives: 42.3 us -> none  [body(): lax.all_to_all(outgoing, 'expert', split_axis=0, concat_axis=0, tiled=True)]
    reduce_scatter x1 -> x0, waiting for transfers between devices: 41.6 us -> none  [body(): lax.psum_scatter(partial_value, 'head', scatter_dimension=2, tiled=True)]
    all_to_all x1 -> x0, waiting for transfers between devices: 19 us -> none  [body(): lax.all_to_all(summed.astype(jnp.bfloat16), 'expert', split_axis=0, conca...]
    all_gather x2 -> x0, blocking collectives: 11.6 us -> none  [the longest x1 7.39 us: body(): lax.all_gather(scaled, 'head', axis=1, tiled=True)]
    dot_general x4 -> x1, matrix products: 13.6 us -> 2.48 us  [body(): jnp.einsum('td,dcj->tcj', restored, weight, preferred_element_type=F32)]
    all_to_all x1 -> x0, starting transfers between devices: 6.04 us -> none  [body(): lax.all_to_all(summed.astype(jnp.bfloat16), 'expert', split_axis=0, conca...]
    reduce_sum x5 -> x0, other arithmetic: 3.97 us -> none  [the longest x1 1.33 us: body(): encoded = own_cols + jnp.sum(gates[:, :, None] * picked, axis=1)]
  transfers between devices with their start and end apart: 3 -> 1, of which waited for: 2 -> 0; matrix products, arithmetic and copies ran while one was open for 6% -> 4% of each run, Pallas kernels for 0% -> 77%
where the time goes in v1:
time: 99 us; the launch traced here: 98.7 us
  Pallas kernels  76 us (77%)
  between operations  13.4 us (14%)
  local copies, waits for them, and re-layouts  5.96 us (6%)
  matrix products  2.48 us (3%)
    pallas_call x1, Pallas kernels, encoder(): pl.pallas_call(functools.partial(kernel, n, cap, groups), out_shape=jax.S...  76 us
    unnamed x3, local copies, waits for them, and re-layouts  4.63 us
    dot_general x1, matrix products, body(): jnp.einsum('td,dcj->tcj', restored, weight, preferred_element_type=F32)  2.48 us
  transfers between devices with their start and end apart: 1, of which 0 were waited for; matrix products, arithmetic and copies ran while one was open for 4% of the time, Pallas kernels for 77%

profile of v1, /device:TPU:16, one launch (start us, length us, event | category | flops | bytes accessed | tf_op | source)
XLA Modules:
  0.0 98.7 jit_solution(3296913714130275316)
XLA Ops:
  6.5 0.0 all-gather.2.cloned.1.call-start
  6.5 1.6 %copy.14 = bf16[64,2,512]{2,0,1:T(8,128)(2,1)} copy(bf16[64,2,512]{2,1,0:T(2,128)(2,1)} %param.13) | data formatting | bytes 262144 | tf_op args[6]
  8.1 0.0 all-gather.2.cloned.1.call-update
  8.1 1.5 %copy.13.routes_ref = s32[256,2]{1,0:T(8,128)} copy(s32[256,2]{0,1:T(2,128)} %param.9) | data formatting | bytes 4096 | tf_op args[2]
  9.6 1.6 %copy.12.router_ref = bf16[1024,16]{1,0:T(8,128)(2,1)} copy(bf16[1024,16]{0,1:T(8,128)(2,1)} %param.8) | data formatting | bytes 65536 | tf_op args[1]
  11.2 0.7 fusion.2
  11.9 76.0 %shard_map.73 = bf16[256,1024]{1,0:T(8,128)(2,1)} custom-call(bf16[256,1024]{1,0:T(8,128)(2,1)} %tokens_ref.1, bf16[1024,16]{1,0:T(8,128)(2,1)} %copy.12.router_ref, s32[256,2]{1,0:T(8,128)} %copy.13.routes_ref, bf16[1,1024,2048]{2,1,0:T(8,128)(2,1)} %w_in_hbm.1, bf16[1,2048,1024]{2,1,0:T(8,128)(2,1)} %w_out_hbm.1), custom_call_target="tpu_custom_call" | custom-call | flops 6442450944 | bytes 8388608 | tf_op jit(solution)/shard_map/pallas_call | solution.py:254
  88.0 0.0 all-gather.2.cloned.1.call-done
  88.0 2.5 %fusion = bf16[256,2,512]{2,0,1:T(8,128)(2,1)S(1)} fusion(bf16[1024,2,512]{2,0,1:T(8,128)(2,1)} %all-gather.2.cloned.1.call-done, bf16[256,1024]{1,0:T(8,128)(2,1)} %shard_map.73, f32[256]{0:T(256)S(1)} %compare_convert_fusion), kind=kOutput, calls=%fused_computation.1 | convolution fusion | flops 537395200 | bytes 3146752 | tf_op jit(solution)/shard_map/td,dcj->tcj/dot_general | solution.py:292
  90.5 1.3 %copy.15 = bf16[256,2,512]{2,1,0:T(2,128)(2,1)} copy(bf16[256,2,512]{2,0,1:T(8,128)(2,1)S(1)} %fusion) | data formatting | bytes 1048576 | tf_op jit(solution)/shard_map/convert_element_type | solution.py:300
  (2 shorter events, 0.0 us)
Async XLA Ops:
  6.5 81.5 %all-gather.2.cloned.1.call-start = ((), (), s32[]{:S(2)}) async-start(), calls=%async_computation | async-start | bytes 2228224 | tf_op jit(solution)/shard_map/all_gather | solution.py:290
Sparse Core Ops, SparseCore 0:
  9.5 51.7 all-gather.1

commit v2 on v1

--- a/solution.py
+++ b/solution.py
@@ -25,10 +25,10 @@
 
 
 def kernel(
-    n, cap, groups,
-    tokens_ref, router_ref, routes_ref, w_in_hbm, w_out_hbm, restored_ref,
-    w_in, w_out, onehots, outgoing, rows_in, hidden, part_out, part_in, part_own, summed, back, coded,
-    w_sem, disp_send, disp_recv, fwd_send, fwd_recv, red_send, red_recv, ret_send, ret_recv, code_send, code_recv,
+    n, cap, spans,
+    tokens_ref, router_ref, routes_ref, lengths_ref, kv_hbm, w_in_hbm, w_out_hbm, kv_ref,
+    w_in, w_out, onehots, outgoing, rows_in, hidden, part_out, part_in, part_own, summed, back, coded, kv_all, part_kv,
+    w_sem, disp_send, disp_recv, fwd_send, fwd_recv, red_send, red_recv, ret_send, ret_recv, code_send, code_recv, kv_send, kv_recv,
 ):
     me = lax.axis_index("expert")
     head = lax.axis_index("head")
@@ -36,13 +36,20 @@
     count, width = tokens_ref.shape
     half = width // 2
     ff = w_in.shape[1]
-    block = n // groups * cap
+    groups = len(spans)
+    depth = kv_hbm.shape[0]
     near = n // 2
     mine = pl.ds(pl.multiple_of(head * half, half), half)
     theirs = pl.ds(pl.multiple_of(other * half, half), half)
 
     load_in = pltpu.make_async_copy(w_in_hbm.at[0], w_in, w_sem.at[0])
     load_out = pltpu.make_async_copy(w_out_hbm.at[0], w_out, w_sem.at[1])
+
+    def kv_at(expert):
+        return pl.ds(pl.multiple_of(expert * depth, depth), depth)
+
+    load_kv = pltpu.make_async_copy(kv_hbm, kv_all.at[kv_at(me)], w_sem.at[2])
+    load_kv.start()
     load_in.start()
     load_out.start()
 
@@ -53,20 +60,51 @@
         pl.semaphore_signal(barrier, inc=1, device_id={"expert": flip(me, k, n)}, device_id_type=MESH)
 
     pl.semaphore_signal(barrier, inc=1, device_id={"head": other}, device_id_type=MESH)
+
+    load_kv.wait()
+    pl.semaphore_wait(barrier, n)
+
+    def kv_copy(bit, i):
+        owner = flip(me, i * (2 * bit), n)
+        sem = n // (2 * bit) - 1 + i
+        return pltpu.make_async_remote_copy(
+            src_ref=kv_all.at[kv_at(owner)], dst_ref=kv_all.at[kv_at(owner)],
+            send_sem=kv_send.at[sem], recv_sem=kv_recv.at[sem],
+            device_id={"expert": flip(me, bit, n)}, device_id_type=MESH,
+        )
+
+    def kv_start(bit):
+        @pl.loop(0, n // (2 * bit))
+        def _(i):
+            kv_copy(bit, i).start()
+
+    def kv_wait(bit):
+        @pl.loop(0, n // (2 * bit))
+        def _(i):
+            kv_copy(bit, i).wait_recv()
+
+    bits = []
+    while n >> (len(bits) + 1):
+        bits.append(n >> (len(bits) + 1))
+    kv_start(bits[0])
 
     wide = tokens_ref[...].astype(F32)
     center = jnp.mean(wide, axis=-1, keepdims=True)
     spread = jnp.mean((wide - center) ** 2, axis=-1, keepdims=True)
     normed = ((wide - center) * lax.rsqrt(spread + 1e-05)).astype(BF16)
-    logits = jnp.dot(normed, router_ref[...], preferred_element_type=F32)
-    route0 = routes_ref[:, 0:1]
-    route1 = routes_ref[:, 1:2]
+    logits = lax.dot_general(normed, router_ref[...], (((1,), (1,)), ((), ())), preferred_element_type=F32)
+    across = lax.broadcasted_iota(jnp.int32, (count, count), 1)
+    down = lax.broadcasted_iota(jnp.int32, (count, count), 0)
+
+    def column(row):
+        return jnp.sum(jnp.where(across == down, row.astype(F32), 0.0), axis=1, keepdims=True).astype(jnp.int32)
+
+    route0 = column(routes_ref[0:1, :])
+    route1 = column(routes_ref[1:2, :])
     ids = lax.broadcasted_iota(jnp.int32, (count, n), 1)
     hot0 = (ids == route0).astype(F32)
     hot1 = (ids == route1).astype(F32)
-    earlier = (
-        lax.broadcasted_iota(jnp.int32, (count, count), 1) < lax.broadcasted_iota(jnp.int32, (count, count), 0)
-    ).astype(F32).astype(BF16)
+    earlier = (across < down).astype(F32).astype(BF16)
     before = jnp.dot(earlier, (hot0 + hot1).astype(BF16), preferred_element_type=F32)
     slot0 = jnp.sum(before * hot0, axis=1, keepdims=True).astype(jnp.int32)
     slot1 = jnp.sum(before * hot1, axis=1, keepdims=True).astype(jnp.int32)
@@ -105,7 +143,6 @@
         )
 
     packed(near, n)
-    pl.semaphore_wait(barrier, n)
 
     @pl.loop(near, n)
     def _(k):
@@ -123,10 +160,8 @@
     onehots[...] = low.astype(BF16)
     rest = (low - low.astype(BF16).astype(F32)).astype(BF16)
 
-    per = n // groups
-
     def span(g):
-        return slice(g * block, (g + 1) * block)
+        return slice(spans[g][0] * cap, spans[g][1] * cap)
 
     def forward_copy(g):
         return pltpu.make_async_remote_copy(
@@ -150,9 +185,9 @@
         )
 
     def arrive(g):
-        far = g * per >= near
-
-        @pl.loop(max(1, g * per), (g + 1) * per)
+        far = spans[g][0] >= near
+
+        @pl.loop(max(1, spans[g][0]), spans[g][1])
         def _(k):
             (far_copy if far else near_copy)(k).wait_recv()
 
@@ -162,21 +197,22 @@
     def work(g):
         if g == 0:
             load_in.wait()
-        if g * per >= near:
+        if spans[g][0] >= near:
             forward_copy(g).wait_recv()
         tile = ff // 4
+        size = (spans[g][1] - spans[g][0]) * cap
 
         @pl.loop(0, 4)
         def _(i):
             cols = pl.ds(pl.multiple_of(i * tile, tile), tile)
             value = jnp.dot(rows_in[span(g), :], w_in[:, cols], preferred_element_type=F32)
-            hidden[:, cols] = jnp.maximum(value, 0.0).astype(BF16)
+            hidden[:size, cols] = jnp.maximum(value, 0.0).astype(BF16)
 
         if g == 0:
             load_out.wait()
-        part_out[span(g), :] = jnp.dot(hidden[...], w_out[:, theirs], preferred_element_type=F32).astype(BF16)
+        part_out[span(g), :] = jnp.dot(hidden[:size, :], w_out[:, theirs], preferred_element_type=F32).astype(BF16)
         reduce_copy(g).start()
-        part_own[span(g), :] = jnp.dot(hidden[...], w_out[:, mine], preferred_element_type=F32)
+        part_own[span(g), :] = jnp.dot(hidden[:size, :], w_out[:, mine], preferred_element_type=F32)
 
     def give(g):
         reduce_copy(g).wait_recv()
@@ -184,7 +220,7 @@
         if g == 0:
             back[0:cap, :] = summed[0:cap, :]
 
-        @pl.loop(max(1, g * per), (g + 1) * per)
+        @pl.loop(max(1, spans[g][0]), spans[g][1])
         def _(k):
             return_copy(k).start()
 
@@ -192,11 +228,18 @@
     work(0)
     arrive(1)
     for g in range(1, groups):
+        if g < len(bits):
+            kv_wait(bits[g - 1])
+            kv_start(bits[g])
         if g + 1 < groups:
             arrive(g + 1)
         work(g)
         give(g - 1)
     give(groups - 1)
+    for g in range(groups, len(bits)):
+        kv_wait(bits[g - 1])
+        kv_start(bits[g])
+    kv_wait(bits[-1])
 
     @pl.loop(1, n)
     def _(k):
@@ -219,6 +262,13 @@
         device_id={"head": other}, device_id_type=MESH,
     )
     swap.start()
+    position = lax.broadcasted_iota(jnp.int32, (count, 1), 0)
+    limit = jnp.zeros((count, 1), jnp.int32)
+    for i in range(lengths_ref.shape[0]):
+        inside = (position >= i * SLEN) & (position < (i + 1) * SLEN)
+        limit = jnp.where(inside, i * SLEN + lengths_ref[i], limit)
+    keep = (position < limit).astype(F32)
+    part_kv[...] = jnp.dot(coded[:, mine], kv_all[mine, :], preferred_element_type=F32)
 
     @pl.loop(1, near)
     def _(k):
@@ -233,28 +283,40 @@
         return_copy(k).wait_send()
 
     for g in range(groups):
-        if g * per >= near:
+        if spans[g][0] >= near:
             forward_copy(g).wait_send()
         reduce_copy(g).wait_send()
+
+    for bit in bits:
+
+        @pl.loop(0, n // (2 * bit))
+        def _(i, bit=bit):
+            kv_copy(bit, i).wait_send()
+
     swap.wait()
-    restored_ref[...] = coded[...]
-
-
-def encoder(tokens, router, routes, w_in, w_out):
+    total = part_kv[...] + jnp.dot(coded[:, theirs], kv_all[theirs, :], preferred_element_type=F32)
+    kv_ref[...] = (total * keep).astype(BF16)
+
+
+def encoder(tokens, router, routes, lengths, kv_weight, w_in, w_out):
     n = lax.axis_size("expert")
     count, width = tokens.shape
     half = width // 2
     ff = w_in.shape[2]
     cap = -(-(3 * count // n) // 16) * 16
-    groups = 4
+    spans = [(0, n // 4), (n // 4, n // 2)]
+    spans += [(n // 2 + i * n // 8, n // 2 + (i + 1) * n // 8) for i in range(4)]
+    groups = len(spans)
     slots = n * cap
     vmem = pl.BlockSpec(memory_space=pltpu.VMEM)
     anywhere = pl.BlockSpec(memory_space=pl.ANY)
     dma = pltpu.SemaphoreType.DMA
     return pl.pallas_call(
-        functools.partial(kernel, n, cap, groups),
-        out_shape=jax.ShapeDtypeStruct((count, width), BF16),
-        in_specs=[vmem, vmem, vmem, anywhere, anywhere],
+        functools.partial(kernel, n, cap, spans),
+        out_shape=jax.ShapeDtypeStruct((count, kv_weight.shape[1]), BF16),
+        in_specs=[
+            vmem, vmem, vmem, pl.BlockSpec(memory_space=pltpu.SMEM), anywhere, anywhere, anywhere
+        ],
         out_specs=vmem,
         scratch_shapes=[
             pltpu.VMEM((width, ff), BF16),
@@ -262,19 +324,22 @@
             pltpu.VMEM((count, slots), BF16),
             pltpu.VMEM((slots, width), BF16),
             pltpu.VMEM((slots, width), BF16),
-            pltpu.VMEM((slots // groups, ff), BF16),
+            pltpu.VMEM((slots // 4, ff), BF16),
             pltpu.VMEM((slots, half), BF16),
             pltpu.VMEM((slots, half), BF16),
             pltpu.VMEM((slots, half), F32),
             pltpu.VMEM((slots, half), BF16),
             pltpu.VMEM((slots, half), BF16),
             pltpu.VMEM((count, width), BF16),
-            dma((2,)),
+            pltpu.VMEM((width, kv_weight.shape[1]), BF16),
+            pltpu.VMEM((count, kv_weight.shape[1]), F32),
+            dma((3,)),
             dma((n,)), dma((n,)),
             dma((groups,)), dma((groups,)),
             dma((groups,)), dma((groups,)),
             dma((n,)), dma((n,)),
             dma, dma,
+            dma((n - 1,)), dma((n - 1,)),
         ],
         compiler_params=pltpu.CompilerParams(
             collective_id=0, has_side_effects=True, vmem_limit_bytes=58 * 1024 * 1024
@@ -282,22 +347,14 @@
         cost_estimate=pl.CostEstimate(
             flops=4 * slots * width * ff, bytes_accessed=4 * width * ff, transcendentals=0
         ),
-    )(tokens, router, routes, w_in, w_out)
+    )(tokens, router.T, routes.T, lengths, kv_weight, w_in, w_out)
 
 
 def body(tokens, router, routes, w_in, w_out, lengths, kv_weight):
     count = tokens.shape[0]
-    weight = lax.all_gather(kv_weight, "expert", axis=0, tiled=True)
-    restored = encoder(tokens, router, routes, w_in, w_out)
-    projected = jnp.einsum("td,dcj->tcj", restored, weight, preferred_element_type=F32)
-    place = jnp.arange(count, dtype=jnp.int32)
-    sentence = place // SLEN
-    pick_len = (sentence[:, None] == jnp.arange(lengths.shape[0], dtype=jnp.int32)[None, :]).astype(
-        jnp.int32
-    )
-    limit = jnp.sum(pick_len * lengths[None, :], axis=1)
-    keep = (place % SLEN < limit).astype(F32)
-    return (projected * keep[:, None, None]).astype(BF16)
+    flat = kv_weight.reshape(kv_weight.shape[0], -1)
+    out = encoder(tokens, router, routes, lengths, flat, w_in, w_out)
+    return out.reshape((count,) + kv_weight.shape[1:])
 
 
 def solution(mesh):

time: 99 us -> 85.7 us (0.87)
  between operations: 13.4 us -> 0.01 us
  Pallas kernels: 76 us -> 81.7 us
  matrix products: 2.48 us -> 0 us
  local copies, waits for them, and re-layouts: 5.96 us -> 3.79 us
    pallas_call x1, Pallas kernels: 76 us -> 81.7 us  [encoder(): pl.pallas_call(functools.partial(kernel, n, cap, spans), out_shape=jax.Sh...]
    unnamed x3 -> x1, local copies, waits for them, and re-layouts: 4.63 us -> 1.57 us
    dot_general x1 -> x0, matrix products: 2.48 us -> none  [body(): jnp.einsum('td,dcj->tcj', restored, weight, preferred_element_type=F32)]
    reshape x0 -> x1, local copies, waits for them, and re-layouts: none -> 2.22 us  [body(): return out.reshape((count,) + kv_weight.shape[1:])]
    convert_element_type x1 -> x0, local copies, waits for them, and re-layouts: 1.33 us -> none  [body(): return (projected * keep[:, None, None]).astype(BF16)]
  transfers between devices with their start and end apart: 1 -> 0, of which waited for: 0 -> 0; matrix products, arithmetic and copies ran while one was open for 4% -> 0% of each run, Pallas kernels for 77% -> 0%
where the time goes in v2:
time: 85.7 us; the launch traced here: 85.5 us
  Pallas kernels  81.7 us (95%)
  local copies, waits for them, and re-layouts  3.79 us (4%)
    pallas_call x1, Pallas kernels, encoder(): pl.pallas_call(functools.partial(kernel, n, cap, spans), out_shape=jax.Sh...  81.7 us
    reshape x1, local copies, waits for them, and re-layouts, body(): return out.reshape((count,) + kv_weight.shape[1:])  2.22 us

profile of v2, /device:TPU:16, one launch (start us, length us, event | category | flops | bytes accessed | tf_op | source)
XLA Modules:
  0.0 85.5 jit_solution(16162596560681095111)
XLA Ops:
  0.0 1.6 %copy.8 = bf16[8,8,2,512]{3,1,2,0:T(8,128)(2,1)} copy(bf16[8,8,2,512]{3,2,1,0:T(2,128)(2,1)} %bitcast.4) | data formatting | bytes 262144
  1.6 81.7 %shard_map.73 = bf16[256,1024]{1,0:T(8,128)(2,1)} custom-call(bf16[256,1024]{1,0:T(8,128)(2,1)} %tokens_ref.1, bf16[16,1024]{1,0:T(8,128)(2,1)} %bitcast.6, s32[2,256]{1,0:T(2,128)} %bitcast.7, s32[2]{0:T(128)} %lengths_ref.1, bf16[64,1024]{1,0:T(8,128)(2,1)} %bitcast.5, bf16[1,1024,2048]{2,1,0:T(8,128)(2,1)} %w_in_hbm.1, bf16[1,2048,1024]{2,1,0:T(8,128)(2,1)} %w_out_hbm.1), custom_call_target="tpu_custom_call" | custom-call | flops 6442450944 | bytes 8388608 | tf_op jit(solution)/shard_map/pallas_call | solution.py:314
  83.3 2.2 %reshape.7 = bf16[256,2,512]{2,1,0:T(2,128)(2,1)} reshape(bf16[256,1024]{1,0:T(8,128)(2,1)} %shard_map.73) | data formatting | bytes 1048576 | tf_op jit(solution)/shard_map/reshape | solution.py:357

commit v3 on v2

--- a/solution.py
+++ b/solution.py
@@ -144,15 +144,15 @@
 
     packed(near, n)
 
+    packed(0, near)
+
+    @pl.loop(1, near)
+    def _(k):
+        near_copy(k).start()
+
     @pl.loop(near, n)
     def _(k):
         far_copy(k).start()
-
-    packed(0, near)
-
-    @pl.loop(1, near)
-    def _(k):
-        near_copy(k).start()
 
     rows_in[0:cap, :] = outgoing[0:cap, :]
 

time: 85.7 us -> 84.4 us (0.985)
  Pallas kernels: 81.7 us -> 80.3 us
    pallas_call x1, Pallas kernels: 81.7 us -> 80.3 us  [encoder(): pl.pallas_call(functools.partial(kernel, n, cap, spans), out_shape=jax.Sh...]
where the time goes in v3:
time: 84.4 us; the launch traced here: 84.1 us
  Pallas kernels  80.3 us (95%)
  local copies, waits for them, and re-layouts  3.79 us (4%)
    pallas_call x1, Pallas kernels, encoder(): pl.pallas_call(functools.partial(kernel, n, cap, spans), out_shape=jax.Sh...  80.3 us
    reshape x1, local copies, waits for them, and re-layouts, body(): return out.reshape((count,) + kv_weight.shape[1:])  2.22 us

profile of v3, /device:TPU:16, one launch (start us, length us, event | category | flops | bytes accessed | tf_op | source)
XLA Modules:
  0.0 84.1 jit_solution(10653538725075534299)
XLA Ops:
  0.0 1.6 %copy.8 = bf16[8,8,2,512]{3,1,2,0:T(8,128)(2,1)} copy(bf16[8,8,2,512]{3,2,1,0:T(2,128)(2,1)} %bitcast.4) | data formatting | bytes 262144
  1.6 80.3 %shard_map.73 = bf16[256,1024]{1,0:T(8,128)(2,1)} custom-call(bf16[256,1024]{1,0:T(8,128)(2,1)} %tokens_ref.1, bf16[16,1024]{1,0:T(8,128)(2,1)} %bitcast.6, s32[2,256]{1,0:T(2,128)} %bitcast.7, s32[2]{0:T(128)} %lengths_ref.1, bf16[64,1024]{1,0:T(8,128)(2,1)} %bitcast.5, bf16[1,1024,2048]{2,1,0:T(8,128)(2,1)} %w_in_hbm.1, bf16[1,2048,1024]{2,1,0:T(8,128)(2,1)} %w_out_hbm.1), custom_call_target="tpu_custom_call" | custom-call | flops 6442450944 | bytes 8388608 | tf_op jit(solution)/shard_map/pallas_call | solution.py:314
  81.9 2.2 %reshape.7 = bf16[256,2,512]{2,1,0:T(2,128)(2,1)} reshape(bf16[256,1024]{1,0:T(8,128)(2,1)} %shard_map.73) | data formatting | bytes 1048576 | tf_op jit(solution)/shard_map/reshape | solution.py:357
